TPU v7x, 128 devices: a whole 4x4x4 slice. The times are simulated.
128 devices in a mesh: dp: 64 (over z, x, y_lo, core), blk: 2 (over y_hi).
Axes of the slice: x: 4, y: 4 (y_hi: 2, y_lo: 2; y = y_hi * 2 + y_lo), z: 4, core: 2. Of those that a mesh axis runs over, the one named last changes fastest.
Arguments:
- inputs: bfloat16 [64, 256, 1152], P('dp', 'blk'), may hold values from -6 to 6
- text: bfloat16 [64, 32, 4096], P('dp', 'blk'), may hold values from -6 to 6
- masked: int32 [64, 256], P('dp', 'blk'), may hold values from 0 to 1, as said below
- cot: bfloat16 [64, 256, 1152], P('dp', 'blk'), may hold values from -6 to 6
- norm_gains: bfloat16 [3, 1152], P(None, ('dp', 'blk')), may hold values from 0.5 to 1.5
- norm_biases: bfloat16 [3, 1152], P(None, ('dp', 'blk')), may hold values from -2 to 2
- w_qkv: bfloat16 [1152, 3456], P(('dp', 'blk')), may hold values from -0.1875 to 0.1875
- w_out: bfloat16 [1152, 1152], P(('dp', 'blk')), may hold values from -0.75 to 0.75
- w_text: bfloat16 [4096, 1152], P(('dp', 'blk')), may hold values from -0.09375 to 0.09375
- w_query: bfloat16 [1152, 1152], P(('dp', 'blk')), may hold values from -0.1875 to 0.1875
- w_memory: bfloat16 [1152, 2304], P(('dp', 'blk')), may hold values from -0.1875 to 0.1875
- w_cross_out: bfloat16 [1152, 1152], P(('dp', 'blk')), may hold values from -0.375 to 0.375
- w_up: bfloat16 [1152, 4608], P(('dp', 'blk')), may hold values from -0.1875 to 0.1875
- up_bias: bfloat16 [4608], P(('dp', 'blk')), may hold values from -2 to 2
- w_down: bfloat16 [4608, 1152], P(('dp', 'blk')), may hold values from -0.09375 to 0.09375
- down_bias: bfloat16 [1152], P(('dp', 'blk')), may hold values from -2 to 2
Outputs:
- block_output: bfloat16 [64, 256, 1152], P('dp', 'blk')
- input_grads: float32 [64, 256, 1152], P('dp', 'blk')
- norm_gains_grad: float32 [3, 1152], P(None, ('dp', 'blk'))
- norm_biases_grad: float32 [3, 1152], P(None, ('dp', 'blk'))
- w_qkv_grad: float32 [1152, 3456], P(('dp', 'blk'))
- w_out_grad: float32 [1152, 1152], P(('dp', 'blk'))
- w_text_grad: float32 [4096, 1152], P(('dp', 'blk'))
- w_query_grad: float32 [1152, 1152], P(('dp', 'blk'))
- w_memory_grad: float32 [1152, 2304], P(('dp', 'blk'))
- w_cross_out_grad: float32 [1152, 1152], P(('dp', 'blk'))
- w_up_grad: float32 [1152, 4608], P(('dp', 'blk'))
- up_bias_grad: float32 [4608], P(('dp', 'blk'))
- w_down_grad: float32 [4608, 1152], P(('dp', 'blk'))
- down_bias_grad: float32 [1152], P(('dp', 'blk'))
Inputs may be any that keep to these rules, and one draw needn't show every extreme that they name: For each image, masked holds 4 * 2**e ones, e drawn evenly from 0 to 6 and the count capped at 256, at positions drawn afresh.
All inputs are finite; a program needn't handle non-finite values.
Results may differ from a plain program's by a relative error of at most 0.024.
Values may be sent and summed in bfloat16 or wider, within the bound.
No kernel may reach another device: no remote copies, remote signals or barrier semaphores. Data moves between devices by JAX's collectives and lax.ppermute only.
A program may use at most 384 MiB of HBM per device.

v0:
```python
import jax
import jax.numpy as jnp
from jax import lax
from jax.sharding import PartitionSpec as P

HEAD = 72


def normalize(values, gain, shift):
    center = values - jnp.mean(values, -1, keepdims=True)
    spread = jnp.mean(center * center, -1, keepdims=True)
    return center * lax.rsqrt(spread + 1e-05) * gain + shift


def norm_back(values, gain, shift, upstream):
    result, pull = jax.vjp(normalize, values, gain, shift)
    return pull(upstream)


def attend(queries, keys, values, score_scale):
    scores = (
        jnp.einsum("iqhd,ikhd->ihqk", queries, keys, preferred_element_type=jnp.float32)
        * score_scale
    )
    highest = jnp.max(scores, -1, keepdims=True)
    log_total = highest + jnp.log(jnp.sum(jnp.exp(scores - highest), -1, keepdims=True))
    probs = jnp.exp(scores - log_total).astype(jnp.bfloat16)
    mixed = jnp.einsum("ihqk,ikhd->iqhd", probs, values, preferred_element_type=jnp.float32)
    return (mixed.astype(jnp.bfloat16), log_total)


def attend_back(queries, keys, values, log_total, upstream, score_scale):
    scores = (
        jnp.einsum("iqhd,ikhd->ihqk", queries, keys, preferred_element_type=jnp.float32)
        * score_scale
    )
    probs = jnp.exp(scores - log_total)
    probs_grad = jnp.einsum("iqhd,ikhd->ihqk", upstream, values, preferred_element_type=jnp.float32)
    value_grad = jnp.einsum(
        "ihqk,iqhd->ikhd", probs.astype(jnp.bfloat16), upstream, preferred_element_type=jnp.float32
    )
    scores_grad = (probs * (probs_grad - jnp.sum(probs * probs_grad, -1, keepdims=True))).astype(
        jnp.bfloat16
    )
    query_grad = (
        jnp.einsum("ihqk,ikhd->iqhd", scores_grad, keys, preferred_element_type=jnp.float32)
        * score_scale
    ).astype(jnp.bfloat16)
    key_grad = (
        jnp.einsum("ihqk,iqhd->ikhd", scores_grad, queries, preferred_element_type=jnp.float32)
        * score_scale
    )
    return (query_grad, key_grad, value_grad)


def per_device(
    inputs,
    text,
    masked,
    cot,
    norm_gains,
    norm_biases,
    w_qkv,
    w_out,
    w_text,
    w_query,
    w_memory,
    w_cross_out,
    w_up,
    up_bias,
    w_down,
    down_bias,
):
    images, tok_rows, model_width = inputs.shape
    head_count = model_width // HEAD
    score_scale = HEAD ** (-0.5)

    def heads_of(values):
        return values.reshape(images, values.shape[1], head_count, HEAD)

    resid = inputs.astype(jnp.float32)
    block_set = (
        lax.all_gather(norm_gains, ("dp", "blk"), axis=1, tiled=True),
        lax.all_gather(norm_biases, ("dp", "blk"), axis=1, tiled=True),
        lax.all_gather(w_qkv, ("dp", "blk"), axis=0, tiled=True),
        lax.all_gather(w_out, ("dp", "blk"), axis=0, tiled=True),
        lax.all_gather(w_text, ("dp", "blk"), axis=0, tiled=True),
        lax.all_gather(w_query, ("dp", "blk"), axis=0, tiled=True),
        lax.all_gather(w_memory, ("dp", "blk"), axis=0, tiled=True),
        lax.all_gather(w_cross_out, ("dp", "blk"), axis=0, tiled=True),
    )
    (
        gathered_gains,
        gathered_shifts,
        joined_weight,
        out_weight,
        text_weight,
        query_weight,
        memory_weight,
        cross_weight,
    ) = block_set
    gains = gathered_gains.astype(jnp.float32)
    shifts = gathered_shifts.astype(jnp.float32)
    first = normalize(resid, gains[0], shifts[0]).astype(jnp.bfloat16)
    joined = jnp.einsum(
        "isd,de->ise", first, joined_weight, preferred_element_type=jnp.float32
    ).astype(jnp.bfloat16)
    queries = heads_of(joined[..., :model_width])
    keys_local = heads_of(joined[..., model_width : 2 * model_width])
    values_local = heads_of(joined[..., 2 * model_width :])
    keys, values = (
        lax.all_gather(keys_local, "blk", axis=1, tiled=True),
        lax.all_gather(values_local, "blk", axis=1, tiled=True),
    )
    attended, self_total = attend(queries, keys, values, score_scale)
    attended = attended.reshape(images, tok_rows, model_width)
    second = resid + jnp.einsum(
        "isd,de->ise", attended, out_weight, preferred_element_type=jnp.float32
    )
    second_in = normalize(second, gains[1], shifts[1]).astype(jnp.bfloat16)
    cross_queries = jnp.einsum(
        "isd,de->ise", second_in, query_weight, preferred_element_type=jnp.float32
    ).astype(jnp.bfloat16)
    projected = jnp.einsum(
        "itc,cd->itd", text, text_weight, preferred_element_type=jnp.float32
    ).astype(jnp.bfloat16)
    memory_local = jnp.einsum(
        "itd,de->ite", projected, memory_weight, preferred_element_type=jnp.float32
    ).astype(jnp.bfloat16)
    memory = lax.all_gather(memory_local, "blk", axis=1, tiled=True)
    cross_keys = heads_of(memory[..., :model_width])
    cross_values = heads_of(memory[..., model_width:])
    cross_heads = heads_of(cross_queries)
    cross_out, cross_total = attend(cross_heads, cross_keys, cross_values, score_scale)
    cross_out = cross_out.reshape(images, tok_rows, model_width)
    third = second + jnp.einsum(
        "isd,de->ise", cross_out, cross_weight, preferred_element_type=jnp.float32
    )
    third_in = normalize(third, gains[2], shifts[2]).astype(jnp.bfloat16)
    mlp_set = (
        lax.all_gather(w_up, ("dp", "blk"), axis=0, tiled=True),
        lax.all_gather(up_bias, ("dp", "blk"), axis=0, tiled=True),
        lax.all_gather(w_down, ("dp", "blk"), axis=0, tiled=True),
        lax.all_gather(down_bias, ("dp", "blk"), axis=0, tiled=True),
    )
    up_full, up_gathered, down_full, down_gathered = mlp_set
    upward = jnp.einsum(
        "isd,df->isf", third_in, up_full, preferred_element_type=jnp.float32
    ) + up_gathered.astype(jnp.float32)
    hidden = jax.nn.gelu(upward).astype(jnp.bfloat16)
    final = (
        third
        + jnp.einsum("isf,fd->isd", hidden, down_full, preferred_element_type=jnp.float32)
        + down_gathered.astype(jnp.float32)
    )
    block_output = final.astype(jnp.bfloat16)
    pulled = cot.astype(jnp.float32) * masked.astype(jnp.float32)[:, :, None]
    mlp_back = (
        lax.all_gather(w_up, ("dp", "blk"), axis=0, tiled=True),
        lax.all_gather(up_bias, ("dp", "blk"), axis=0, tiled=True),
        lax.all_gather(w_down, ("dp", "blk"), axis=0, tiled=True),
        lax.all_gather(down_bias, ("dp", "blk"), axis=0, tiled=True),
    )
    up_full, up_gathered, down_full, down_gathered = mlp_back
    branch = pulled.astype(jnp.bfloat16)
    down_shift_grad = jnp.sum(branch.astype(jnp.float32), (0, 1))
    down_grad = jnp.einsum("isf,isd->fd", hidden, branch, preferred_element_type=jnp.float32)
    hidden_grad = jnp.einsum("isd,fd->isf", branch, down_full, preferred_element_type=jnp.float32)
    upward_grad = jax.vjp(jax.nn.gelu, upward)[1](hidden_grad)[0].astype(jnp.bfloat16)
    up_shift_grad = jnp.sum(upward_grad.astype(jnp.float32), (0, 1))
    up_grad = jnp.einsum("isd,isf->df", third_in, upward_grad, preferred_element_type=jnp.float32)
    third_in_grad = jnp.einsum(
        "isf,df->isd", upward_grad, up_full, preferred_element_type=jnp.float32
    )
    up_total, up_shift_total, down_total, down_shift_total = (
        lax.psum_scatter(up_grad, ("dp", "blk"), scatter_dimension=0, tiled=True),
        lax.psum_scatter(up_shift_grad, ("dp", "blk"), scatter_dimension=0, tiled=True),
        lax.psum_scatter(down_grad, ("dp", "blk"), scatter_dimension=0, tiled=True),
        lax.psum_scatter(down_shift_grad, ("dp", "blk"), scatter_dimension=0, tiled=True),
    )
    block_back = (
        lax.all_gather(norm_gains, ("dp", "blk"), axis=1, tiled=True),
        lax.all_gather(norm_biases, ("dp", "blk"), axis=1, tiled=True),
        lax.all_gather(w_qkv, ("dp", "blk"), axis=0, tiled=True),
        lax.all_gather(w_out, ("dp", "blk"), axis=0, tiled=True),
        lax.all_gather(w_text, ("dp", "blk"), axis=0, tiled=True),
        lax.all_gather(w_query, ("dp", "blk"), axis=0, tiled=True),
        lax.all_gather(w_memory, ("dp", "blk"), axis=0, tiled=True),
        lax.all_gather(w_cross_out, ("dp", "blk"), axis=0, tiled=True),
    )
    (
        gathered_gains,
        gathered_shifts,
        joined_weight,
        out_weight,
        text_weight,
        query_weight,
        memory_weight,
        cross_weight,
    ) = block_back
    gains = gathered_gains.astype(jnp.float32)
    shifts = gathered_shifts.astype(jnp.float32)
    third_norm_grad, gain_two, shift_two = norm_back(third, gains[2], shifts[2], third_in_grad)
    third_grad = pulled + third_norm_grad
    cross_branch = third_grad.astype(jnp.bfloat16)
    cross_weight_grad = jnp.einsum(
        "isd,ise->de", cross_out, cross_branch, preferred_element_type=jnp.float32
    )
    cross_out_grad = heads_of(
        jnp.einsum(
            "ise,de->isd", cross_branch, cross_weight, preferred_element_type=jnp.float32
        ).astype(jnp.bfloat16)
    )
    cross_query_grad, cross_key_grad, cross_value_grad = attend_back(
        cross_heads, cross_keys, cross_values, cross_total, cross_out_grad, score_scale
    )
    memory_terms = jnp.concatenate(
        [
            cross_key_grad.reshape(images, -1, model_width),
            cross_value_grad.reshape(images, -1, model_width),
        ],
        -1,
    )
    memory_grad = lax.psum_scatter(
        memory_terms.astype(jnp.bfloat16), "blk", scatter_dimension=1, tiled=True
    )
    memory_weight_grad = jnp.einsum(
        "itd,ite->de", projected, memory_grad, preferred_element_type=jnp.float32
    )
    projected_grad = jnp.einsum(
        "ite,de->itd", memory_grad, memory_weight, preferred_element_type=jnp.float32
    ).astype(jnp.bfloat16)
    text_weight_grad = jnp.einsum(
        "itc,itd->cd", text, projected_grad, preferred_element_type=jnp.float32
    )
    query_flat = cross_query_grad.reshape(images, tok_rows, model_width)
    query_weight_grad = jnp.einsum(
        "isd,ise->de", second_in, query_flat, preferred_element_type=jnp.float32
    )
    second_in_grad = jnp.einsum(
        "ise,de->isd", query_flat, query_weight, preferred_element_type=jnp.float32
    )
    second_norm_grad, gain_one, shift_one = norm_back(second, gains[1], shifts[1], second_in_grad)
    second_grad = third_grad + second_norm_grad
    self_branch = second_grad.astype(jnp.bfloat16)
    out_weight_grad = jnp.einsum(
        "isd,ise->de", attended, self_branch, preferred_element_type=jnp.float32
    )
    attended_grad = heads_of(
        jnp.einsum(
            "ise,de->isd", self_branch, out_weight, preferred_element_type=jnp.float32
        ).astype(jnp.bfloat16)
    )
    query_grad, key_grad, value_grad = attend_back(
        queries, keys, values, self_total, attended_grad, score_scale
    )
    key_grad, value_grad = (
        lax.psum_scatter(
            key_grad.astype(jnp.bfloat16), "blk", scatter_dimension=1, tiled=True
        ).astype(jnp.float32),
        lax.psum_scatter(
            value_grad.astype(jnp.bfloat16), "blk", scatter_dimension=1, tiled=True
        ).astype(jnp.float32),
    )
    joined_grad = jnp.concatenate(
        [
            query_grad.reshape(images, tok_rows, model_width),
            key_grad.astype(jnp.bfloat16).reshape(images, tok_rows, model_width),
            value_grad.astype(jnp.bfloat16).reshape(images, tok_rows, model_width),
        ],
        -1,
    )
    joined_weight_grad = jnp.einsum(
        "isd,ise->de", first, joined_grad, preferred_element_type=jnp.float32
    )
    first_grad = jnp.einsum(
        "ise,de->isd", joined_grad, joined_weight, preferred_element_type=jnp.float32
    )
    input_norm_grad, gain_zero, shift_zero = norm_back(resid, gains[0], shifts[0], first_grad)
    input_grads = second_grad + input_norm_grad
    gain_terms = jnp.stack([gain_zero, gain_one, gain_two])
    shift_terms = jnp.stack([shift_zero, shift_one, shift_two])
    (
        gain_total,
        shift_total,
        joined_total,
        out_total,
        text_total,
        query_total,
        memory_total,
        cross_total_grad,
    ) = (
        lax.psum_scatter(gain_terms, ("dp", "blk"), scatter_dimension=1, tiled=True),
        lax.psum_scatter(shift_terms, ("dp", "blk"), scatter_dimension=1, tiled=True),
        lax.psum_scatter(joined_weight_grad, ("dp", "blk"), scatter_dimension=0, tiled=True),
        lax.psum_scatter(out_weight_grad, ("dp", "blk"), scatter_dimension=0, tiled=True),
        lax.psum_scatter(text_weight_grad, ("dp", "blk"), scatter_dimension=0, tiled=True),
        lax.psum_scatter(query_weight_grad, ("dp", "blk"), scatter_dimension=0, tiled=True),
        lax.psum_scatter(memory_weight_grad, ("dp", "blk"), scatter_dimension=0, tiled=True),
        lax.psum_scatter(cross_weight_grad, ("dp", "blk"), scatter_dimension=0, tiled=True),
    )
    return (
        block_output,
        input_grads,
        gain_total,
        shift_total,
        joined_total,
        out_total,
        text_total,
        query_total,
        memory_total,
        cross_total_grad,
        up_total,
        up_shift_total,
        down_total,
        down_shift_total,
    )


def solution(mesh):
    return jax.shard_map(
        per_device,
        mesh=mesh,
        in_specs=(
            P("dp", "blk", None),
            P("dp", "blk", None),
            P("dp", "blk"),
            P("dp", "blk", None),
            P(None, ("dp", "blk")),
            P(None, ("dp", "blk")),
            P(("dp", "blk"), None),
            P(("dp", "blk"), None),
            P(("dp", "blk"), None),
            P(("dp", "blk"), None),
            P(("dp", "blk"), None),
            P(("dp", "blk"), None),
            P(("dp", "blk"), None),
            P(("dp", "blk")),
            P(("dp", "blk"), None),
            P(("dp", "blk")),
        ),
        out_specs=(
            P("dp", "blk", None),
            P("dp", "blk", None),
            P(None, ("dp", "blk")),
            P(None, ("dp", "blk")),
            P(("dp", "blk"), None),
            P(("dp", "blk"), None),
            P(("dp", "blk"), None),
            P(("dp", "blk"), None),
            P(("dp", "blk"), None),
            P(("dp", "blk"), None),
            P(("dp", "blk"), None),
            P(("dp", "blk")),
            P(("dp", "blk"), None),
            P(("dp", "blk")),
        ),
        check_vma=False,
    )
```

profile of v0, /device:TPU:1, one launch (start us, length us, event | category | flops | bytes accessed | tf_op | source)
XLA Modules:
  0.0 4514.2 jit_solution(8566444467334869311)
XLA Ops:
  14.4 69.0 %all-reduce.16 = (bf16[1152]{0:T(1024)(128)(2,1)}, bf16[4608]{0:T(1024)(128)(2,1)S(1)}) all-reduce(bf16[1152]{0:T(1024)(128)(2,1)S(1)} %dynamic-update-slice.1, bf16[4608]{0:T(1024)(128)(2,1)S(1)} %dynamic-update-slice), channel_id=1, replica_groups=mesh['dp'=64,'blk'=2] {'dp','blk'}, use_global_device_ids=true, to_apply=%add.1 | all-reduce | flops 5760 | bytes 23040
  84.1 309.6 %all-gather.1 = bf16[128,9,3]{1,2,0:T(4,128)(2,1)S(1)} all-gather(bf16[1,9,3]{1,2,0:T(4,128)(2,1)} %bitcast.271), channel_id=1, replica_groups=mesh['dp'=64,'blk'=2] {'dp','blk'}, dimensions={0}, use_global_device_ids=true | all-gather | bytes 6966 | tf_op jit(solution)/shard_map/all_gather | solution.py:83
  393.8 312.4 %all-gather.2 = bf16[128,9,3]{1,2,0:T(4,128)(2,1)S(1)} all-gather(bf16[1,9,3]{1,2,0:T(4,128)(2,1)} %bitcast.272), channel_id=1, replica_groups=mesh['dp'=64,'blk'=2] {'dp','blk'}, dimensions={0}, use_global_device_ids=true | all-gather | bytes 6966 | tf_op jit(solution)/shard_map/all_gather | solution.py:84
  720.1 222.7 %all-gather.29.cloned.1.call-done = bf16[128,9,1152]{2,1,0:T(8,128)(2,1)} async-done(((bf16[1,9,1152]{2,1,0:T(8,128)(2,1)}), bf16[128,9,1152]{2,1,0:T(8,128)(2,1)}) %all-gather.29.cloned.1.call-update) | async-done | bytes 2654224 | tf_op jit(solution)/shard_map/all_gather | solution.py:90
  948.6 313.6 %all-gather.25.cloned.1.call-done = bf16[128,9,2304]{2,1,0:T(8,128)(2,1)} async-done(((bf16[1,9,2304]{2,1,0:T(8,128)(2,1)}), bf16[128,9,2304]{2,1,0:T(8,128)(2,1)}) %all-gather.25.cloned.1.call-update) | async-done | bytes 5308432 | tf_op jit(solution)/shard_map/all_gather | solution.py:89
  1262.1 9.0 reshape.632
  1271.2 316.6 %all-gather.21.cloned.1.call-done = bf16[128,9,3456]{2,1,0:T(8,128)(2,1)} async-done(((bf16[1,9,3456]{2,1,0:T(8,128)(2,1)}), bf16[128,9,3456]{2,1,0:T(8,128)(2,1)}) %all-gather.21.cloned.1.call-update) | async-done | bytes 7962640 | tf_op jit(solution)/shard_map/all_gather | solution.py:85
  1587.7 14.4 reshape.628
  1607.6 12.3 all_gather.57
  1619.9 10.7 all_gather.56
  1635.5 272.6 %all-gather.19.cloned.1.call-done = bf16[4096,1152]{1,0:T(8,128)(2,1)} async-done(((bf16[32,1152]{1,0:T(8,128)(2,1)}), bf16[4096,1152]{1,0:T(8,128)(2,1)}) %all-gather.19.cloned.1.call-update) | async-done | bytes 9437200 | tf_op jit(solution)/shard_map/all_gather | solution.py:87
  1930.1 313.0 %all-gather.31.cloned.1.call-done = bf16[128,9,4608]{2,1,0:T(8,128)(2,1)} async-done(((bf16[1,9,4608]{2,1,0:T(8,128)(2,1)}), bf16[128,9,4608]{2,1,0:T(8,128)(2,1)}) %all-gather.31.cloned.1.call-update) | async-done | bytes 10616848 | tf_op jit(solution)/shard_map/all_gather | solution.py:141
  2243.2 17.5 reshape.638
  2267.9 297.9 %all-gather.33.cloned.1.call-done = bf16[128,36,1152]{2,1,0:T(8,128)(2,1)} async-done(((bf16[1,36,1152]{2,1,0:T(8,128)(2,1)}), bf16[128,36,1152]{2,1,0:T(8,128)(2,1)}) %all-gather.33.cloned.1.call-update) | async-done | bytes 10616848 | tf_op jit(solution)/shard_map/all_gather | solution.py:143
  2565.9 16.3 reshape.640
  2582.1 9.4 convert_reduce_fusion
  2591.5 8.6 fusion.34
  2653.5 8.9 fusion.91
  2680.0 8.0 fusion.45
  2688.8 12.8 convolution_bitcast_fusion
  2701.6 19.1 copy.100
  2722.5 11.5 fusion.55
  2734.1 688.9 %fusion = f32[48,1152]{1,0:T(8,128)} fusion(f32[4608,1152]{1,0:T(8,128)} %fusion.55), kind=kCustom, calls=%all-reduce-scatter | all-reduce-scatter fusion | flops 7077889 | bytes 21454848
  3451.3 12.6 collective-permute-start.25
  3497.9 13.1 collective-permute-start.16
  3517.2 20.9 collective-permute-start.14
  3562.9 9.6 collective-permute-start.5
  3578.8 11.3 collective-permute-start.2
  3605.9 56.1 %concatenate.23 = f32[1572,1152]{1,0:T(8,128)} concatenate(f32[36,1152]{1,0:T(8,128)} %collective-permute-done.31, f32[48,1152]{1,0:T(8,128)} %collective-permute-done.30, f32[48,1152]{1,0:T(8,128)} %collective-permute-done.29, f32[48,1152]{1,0:T(8,128)} %collective-permute-done.28, f32[48,1152]{1,0:T(8,128)} %collective-permute-done.27, f32[48,1152]{1,0:T(8,128)} %collective-permute-done.26, ...), dimensions={0} | concatenate | bytes 14487552
  3670.1 73.9 %all-reduce.14 = (f32[3,1152]{1,0:T(4,128)S(1)}, f32[3,1152]{1,0:T(4,128)S(1)}, f32[4608]{0:T(1024)S(1)}, f32[1152]{0:T(1024)S(1)}) all-reduce(f32[3,1152]{1,0:T(4,128)S(1)} %pad_maximum_fusion.1, f32[3,1152]{1,0:T(4,128)S(1)} %pad_maximum_fusion.2, f32[4608]{0:T(1024)S(1)} %copy-done.66, ...), channel_id=5, replica_groups=mesh['dp'=64,'blk'=2] {'dp','blk'}, use_global_device_ids=true, to_apply=%region_23.0.clone | all-reduce | flops 12672 | bytes 101376
  3746.9 77.9 %all-reduce.19.cloned.1.call-done = (f32[1152,3456]{1,0:T(8,128)}, f32[1152,1152]{1,0:T(8,128)}, f32[1152,1152]{1,0:T(8,128)}, f32[1152,2304]{1,0:T(8,128)}, f32[1152,1152]{1,0:T(8,128)}, /*index=5*/f32[1152,4608]{1,0:T(8,128)}) async-done(((f32[1152,3456]{1,0:T(8,128)}, f32[1152,1152]{1,0:T(8,128)}, f32[1152,1152]{1,0:T(8,128)}, f32[1152,2304]{1,0:T(8,128)}, f32[1152,1152]{1,0:T(8,128)}, ...) | async-done | bytes 63701008
  3833.1 674.4 %reduce-scatter.21.cloned.1.call-done = f32[32,1152]{1,0:T(8,128)} async-done(((f32[4096,1152]{1,0:T(8,128)}), f32[32,1152]{1,0:T(8,128)}) %reduce-scatter.21.cloned.1.call-update) | async-done | bytes 147472
  (375 shorter events, 274.3 us)
Async XLA Ops:
  7.2 701.4 %all-gather.23.cloned.1.call-start = ((), (), s32[]{:S(2)}) async-start(), calls=%async_computation.7 | async-start | bytes 4755456 | tf_op jit(solution)/shard_map/all_gather | solution.py:86
  8.0 706.4 %all-gather.27.cloned.1.call-start = ((), (), s32[]{:S(2)}) async-start(), calls=%async_computation.9 | async-start | bytes 4755456 | tf_op jit(solution)/shard_map/all_gather | solution.py:88
  8.7 934.2 %all-gather.29.cloned.1.call-start = ((), (), s32[]{:S(2)}) async-start(), calls=%async_computation.10 | async-start | bytes 4755456 | tf_op jit(solution)/shard_map/all_gather | solution.py:90
  9.4 1252.7 %all-gather.25.cloned.1.call-start = ((), (), s32[]{:S(2)}) async-start(), calls=%async_computation.8 | async-start | bytes 9510912 | tf_op jit(solution)/shard_map/all_gather | solution.py:89
  10.0 1577.7 %all-gather.21.cloned.1.call-start = ((), (), s32[]{:S(2)}) async-start(), calls=%async_computation.6 | async-start | bytes 14266368 | tf_op jit(solution)/shard_map/all_gather | solution.py:85
  10.6 1897.5 %all-gather.19.cloned.1.call-start = ((), (), s32[]{:S(2)}) async-start(), calls=%async_computation.4 | async-start | bytes 9510912 | tf_op jit(solution)/shard_map/all_gather | solution.py:87
  11.2 2232.0 %all-gather.31.cloned.1.call-start = ((), (), s32[]{:S(2)}) async-start(), calls=%async_computation.11 | async-start | bytes 19021824 | tf_op jit(solution)/shard_map/all_gather | solution.py:141
  11.9 2553.9 %all-gather.33.cloned.1.call-start = ((), (), s32[]{:S(2)}) async-start(), calls=%async_computation.12 | async-start | bytes 11888640 | tf_op jit(solution)/shard_map/all_gather | solution.py:143
  12.7 2649.7 %reduce-scatter.15.cloned.1.call-start = ((), (), s32[]{:S(2)}) async-start(), calls=%async_computation.5 | async-start | bytes 221184 | tf_op jit(solution)/shard_map/reduce_scatter | solution.py:224
  2616.3 52.5 %reduce-scatter.19.cloned.1.call-start = ((), (), s32[]{:S(2)}) async-start(), calls=%async_computation.14 | async-start | bytes 884736
  2637.2 40.3 reduce-scatter.17.cloned.1.call-start
  2653.2 1171.6 %all-reduce.19.cloned.1.call-start = ((), (), s32[]{:S(2)}) async-start(), calls=%async_computation.16 | async-start | bytes 127401984
  2688.0 1819.5 %reduce-scatter.21.cloned.1.call-start = ((), (), s32[]{:S(2)}) async-start(), calls=%async_computation.15 | async-start | bytes 19021824
  3423.0 28.3 collective-permute-start.30
  3430.8 33.1 collective-permute-start.29
  3436.1 35.6 collective-permute-start.28
  3443.2 30.5 collective-permute-start.27
  3445.2 31.8 collective-permute-start.26
  3451.3 28.8 collective-permute-start.25
  3480.0 30.9 collective-permute-start.20
  3486.5 30.7 collective-permute-start.19
  3488.5 49.6 %collective-permute-start.18 = (f32[48,1152]{1,0:T(8,128)}, f32[48,1152]{1,0:T(8,128)}, u32[]{:S(2)}, u32[]{:S(2)}) collective-permute-start(f32[48,1152]{1,0:T(8,128)} %fusion), channel_id=1, source_target_pairs={{0,19},{1,20},{2,21},{3,22},{4,23},{5,24},{6,25},{7,26},{8,27},{9,... | collective-permute-start | bytes 663560
  3494.2 45.9 %collective-permute-start.17 = (f32[48,1152]{1,0:T(8,128)}, f32[48,1152]{1,0:T(8,128)}, u32[]{:S(2)}, u32[]{:S(2)}) collective-permute-start(f32[48,1152]{1,0:T(8,128)} %fusion), channel_id=1, source_target_pairs={{0,18},{1,19},{2,20},{3,21},{4,22},{5,23},{6,24},{7,25},{8,26},{9,... | collective-permute-start | bytes 663560
  3497.9 44.2 collective-permute-start.16
  3510.9 36.9 collective-permute-start.15
  3517.2 33.5 collective-permute-start.14
  3552.7 22.7 collective-permute-start.8
  3560.1 30.0 collective-permute-start.6
  3562.9 29.1 collective-permute-start.5
  3572.5 33.3 collective-permute-start.4
  3575.4 30.5 collective-permute-start.3
  3578.8 27.1 collective-permute-start.2
  (96 other events, 10384.8 us)
Sparse Core Ops, SparseCore 0:
  9.7 312.7 all-gather.22
  324.2 309.2 all-gather.26
  635.2 307.5 all-gather.28
  944.4 317.7 all-gather.24
  1263.7 323.9 all-gather.20
  1589.3 318.7 all-gather.18
  1909.8 333.3 all-gather.30
  2244.9 320.9 all-gather.32
  2616.4 13.9 reduce-scatter.14
  2637.3 18.9 reduce-scatter.18
  2658.8 18.6 reduce-scatter.16
  2688.1 1136.7 all-reduce.18
  3827.8 679.5 reduce-scatter.20
where the time goes:
time: 4530 us; the launch traced here: 4510 us
  waiting for transfers between devices  2500 us (55%)
  blocking collectives  1480 us (33%)
  local copies, waits for them, and re-layouts  196 us (4%)
  starting transfers between devices  174 us (4%)
  matrix products  132 us (3%)
    unnamed x3, blocking collectives  832 us
    unnamed x49, waiting for transfers between devices  764 us
    all_gather x1, waiting for transfers between devices, per_device(): lax.all_gather(w_qkv, ('dp', 'blk'), axis=0, tiled=True)  317 us
    all_gather x1, waiting for transfers between devices, per_device(): lax.all_gather(w_memory, ('dp', 'blk'), axis=0, tiled=True)  314 us
    all_gather x1, waiting for transfers between devices, per_device(): lax.all_gather(w_up, ('dp', 'blk'), axis=0, tiled=True)  313 us
    all_gather x1, blocking collectives, per_device(): lax.all_gather(norm_biases, ('dp', 'blk'), axis=1, tiled=True)  312 us
    all_gather x1, blocking collectives, per_device(): lax.all_gather(norm_gains, ('dp', 'blk'), axis=1, tiled=True)  310 us
    all_gather x1, waiting for transfers between devices, per_device(): lax.all_gather(w_down, ('dp', 'blk'), axis=0, tiled=True)  298 us
  transfers between devices with their start and end apart: 45, of which 9 were waited for; matrix products, arithmetic and copies ran while one was open for 21% of the time, Pallas kernels for 0%

commit v1 on v0

v1 whole, which is shorter than its diff:
```python
import jax
import jax.numpy as jnp
from jax import lax
from jax.sharding import Mesh, PartitionSpec as P

HEAD = 72
BF = jnp.bfloat16
F32 = jnp.float32
AXES = ("z", "x", "v", "c", "u")
DP = ("z", "x", "v", "c")
NAMES = {"z": ("z", "c"), "x": ("x", "c"), "y": ("v", "c", "u")}


def normalize(values, gain, shift):
    center = values - jnp.mean(values, -1, keepdims=True)
    spread = jnp.mean(center * center, -1, keepdims=True)
    return center * lax.rsqrt(spread + 1e-05) * gain + shift


def norm_back(values, gain, shift, upstream):
    result, pull = jax.vjp(normalize, values, gain, shift)
    return pull(upstream)


def dot(left, right):
    return jnp.dot(left, right, preferred_element_type=F32)


def dot_nt(left, right):
    return lax.dot_general(left, right, (((1,), (1,)), ((), ())), preferred_element_type=F32)


def dot_tn(left, right):
    return lax.dot_general(left, right, (((0,), (0,)), ((), ())), preferred_element_type=F32)


def attend(queries, keys, values, score_scale):
    scores = jnp.einsum("qhd,khd->hqk", queries, keys, preferred_element_type=F32) * score_scale
    highest = jnp.max(scores, -1, keepdims=True)
    log_total = highest + jnp.log(jnp.sum(jnp.exp(scores - highest), -1, keepdims=True))
    probs = jnp.exp(scores - log_total).astype(BF)
    mixed = jnp.einsum("hqk,khd->qhd", probs, values, preferred_element_type=F32)
    return (mixed.astype(BF), log_total)


def attend_back(queries, keys, values, log_total, upstream, score_scale):
    scores = jnp.einsum("qhd,khd->hqk", queries, keys, preferred_element_type=F32) * score_scale
    probs = jnp.exp(scores - log_total)
    probs_grad = jnp.einsum("qhd,khd->hqk", upstream, values, preferred_element_type=F32)
    value_grad = jnp.einsum("hqk,qhd->khd", probs.astype(BF), upstream, preferred_element_type=F32)
    scores_grad = (probs * (probs_grad - jnp.sum(probs * probs_grad, -1, keepdims=True))).astype(BF)
    query_grad = (
        jnp.einsum("hqk,khd->qhd", scores_grad, keys, preferred_element_type=F32) * score_scale
    ).astype(BF)
    key_grad = jnp.einsum("hqk,qhd->khd", scores_grad, queries, preferred_element_type=F32) * score_scale
    return (query_grad, key_grad, value_grad)


def swap(value):
    return lax.ppermute(value, "c", [(0, 1), (1, 0)])


def position_index(axis, place, core):
    if axis == "y":
        return ((place % 2) * 2 + core) * 2 + place // 2
    return place * 2 + core


def receive(value, axis, step, mirrored=True):
    pairs = []
    for core in range(2):
        own = -step if mirrored and core == 1 else step
        for place in range(4):
            pairs.append(
                (position_index(axis, (place + own) % 4, core), position_index(axis, place, core))
            )
    return lax.ppermute(value, NAMES[axis], pairs)


def place_of(axis):
    if axis == "y":
        return 2 * lax.axis_index("u") + lax.axis_index("v")
    return lax.axis_index(axis)


def sign_of():
    return 1 - 2 * lax.axis_index("c")


def places(axis):
    here, sign = place_of(axis), sign_of()
    mine = [here, (here + sign) % 4, (here - sign) % 4, (here + 2) % 4]
    return mine, [mine[0], mine[2], mine[1], mine[3]]


def by_place(pieces, spots):
    slots = jnp.arange(4).reshape((4,) + (1,) * pieces[0].ndim)
    out = pieces[3][None]
    for piece, spot in zip(pieces[:3], spots[:3]):
        out = jnp.where(slots == spot, piece[None], out)
    return out


def gather_small(value, axis):
    pieces = [
        value,
        receive(value, axis, 1),
        receive(value, axis, -1),
        receive(value, axis, 2, False),
    ]
    return by_place(pieces, places(axis)[0])


def gather_large(value, axis):
    half = value.shape[0] // 2
    first = receive(value, axis, 1)
    second = receive(value, axis, -1)
    far = jnp.concatenate(
        [receive(first[:half], axis, 1), receive(second[half:], axis, -1)], 0
    )
    return [value, first, second, far]


def scatter(pieces, axis):
    own, first, second, far = pieces
    total = own.astype(F32)
    total = total + receive(first.astype(BF), axis, -1).astype(F32)
    total = total + receive(second.astype(BF), axis, 1).astype(F32)
    return total + receive(far.astype(BF), axis, 2, False).astype(F32)


def take(blocks, spot):
    return lax.dynamic_index_in_dim(blocks, spot, 0, keepdims=False)


def scatter_blocks(blocks, axis):
    return scatter([take(blocks, spot) for spot in places(axis)[0]], axis)


class Group:
    def __init__(self, value, axis):
        self.axis = axis
        self.own = gather_large(value, axis)
        self.other = [swap(piece) for piece in self.own]
        self.own_spots, self.other_spots = places(axis)

    def times(self, blocks, other, columns=slice(None)):
        pieces, spots = (self.other, self.other_spots) if other else (self.own, self.own_spots)
        total = 0.0
        for piece, spot in zip(pieces, spots):
            total = total + dot(take(blocks, spot), piece[:, columns])
        return total

    def times_rows(self, blocks, other, rows):
        pieces, spots = (self.other, self.other_spots) if other else (self.own, self.own_spots)
        total = 0.0
        for piece, spot in zip(pieces, spots):
            total = total + dot(take(blocks, spot), piece[rows])
        return total

    def back(self, own, other, columns=slice(None)):
        out = []
        for index, mate in enumerate((0, 2, 1, 3)):
            out.append(
                dot_nt(own, self.own[index][:, columns]) + dot_nt(other, self.other[mate][:, columns])
            )
        return by_place(out, self.own_spots)

    def back_rows(self, value, other, rows):
        pieces, spots = (self.other, self.other_spots) if other else (self.own, self.own_spots)
        return by_place([dot_nt(value, piece[rows]) for piece in pieces], spots)


def pair(left_zero, right_zero, left_one, right_one):
    zero = lax.axis_index("c") == 0
    lefts = jnp.where(zero, left_zero, left_one)
    rights = jnp.where(zero, right_zero, right_one)
    left_out = jnp.where(zero, left_one, left_zero)
    right_out = jnp.where(zero, right_one, right_zero)
    return (
        jnp.concatenate([lefts, swap(left_out)], -2),
        jnp.concatenate([rights, swap(right_out)], -2),
    )


def gradient_pieces(lefts, rights, axis):
    return [dot_tn(take(lefts, spot), rights) for spot in places(axis)[0]]


def per_device(
    inputs,
    text,
    masked,
    cot,
    norm_gains,
    norm_biases,
    w_qkv,
    w_out,
    w_text,
    w_query,
    w_memory,
    w_cross_out,
    w_up,
    up_bias,
    w_down,
    down_bias,
):
    inputs, text, masked, cot = inputs[0], text[0], masked[0], cot[0]
    tokens, width = inputs.shape
    heads = width // HEAD
    wide = w_up.shape[1]
    rows = w_qkv.shape[0]
    scale = HEAD ** (-0.5)
    core = lax.axis_index("c")
    zero = core == 0

    up_sorted = w_up.reshape(rows, 4, 4, 2, 2, 2, 36).transpose(0, 4, 5, 3, 2, 1, 6).reshape(rows, 2, wide // 2)
    half_zero = jnp.concatenate([w_qkv[:, : 2 * width], up_sorted[:, 0], w_out, w_cross_out], 1)
    half_one = jnp.concatenate([w_qkv[:, 2 * width :], w_query, up_sorted[:, 1], w_memory], 1)
    kept = jnp.where(zero, half_zero, half_one)
    came = swap(jnp.where(zero, half_one, half_zero))
    chip = jnp.where(
        jnp.arange(2)[:, None, None] == core, kept[None], came[None]
    ).reshape(2 * rows, -1)
    column = gather_small(chip, "y")
    eight = (
        column.reshape(2, 2, 2, rows, -1).transpose(1, 2, 0, 3, 4).reshape(8 * rows, -1)
    )
    text_down = jnp.concatenate([w_text, w_down], 0)
    text_down = gather_small(text_down, "z")
    text_rows, down_rows = w_text.shape[0], w_down.shape[0]
    text_down = jnp.concatenate(
        [
            text_down[:, :text_rows].reshape(4 * text_rows, width),
            text_down[:, text_rows:].reshape(4 * down_rows, width),
        ],
        0,
    )
    split = 4 * width
    plane = gather_small(eight[:, :split], "x").reshape(32 * rows, split)
    plane_x = gather_small(eight[:, split:], "z").reshape(32 * rows, 2 * width)
    text_down = gather_small(text_down, "x")
    text_down = jnp.concatenate(
        [
            text_down[:, : 4 * text_rows].reshape(16 * text_rows, width),
            text_down[:, 4 * text_rows :].reshape(16 * down_rows, width),
        ],
        0,
    )
    joined_set = Group(plane[:, : 2 * width], "z")
    mixed_set = Group(plane_x, "x")
    low_set = Group(text_down, "y")
    up_set = Group(plane[:, 2 * width :], "z")
    text_part = slice(0, 16 * text_rows)
    down_part = slice(16 * text_rows, None)

    small = jnp.concatenate(
        [norm_gains.reshape(-1), norm_biases.reshape(-1), up_bias, down_bias]
    )
    small = lax.all_to_all(
        jnp.broadcast_to(small, (128, small.shape[0])), AXES, 0, 0, tiled=True
    ).astype(F32)
    gains = small[:, : 3 * rows].reshape(128, 3, rows).transpose(1, 0, 2).reshape(3, width)
    shifts = (
        small[:, 3 * rows : 6 * rows].reshape(128, 3, rows).transpose(1, 0, 2).reshape(3, width)
    )
    up_shift = (
        small[:, 6 * rows : 6 * rows + 36]
        .reshape(4, 4, 2, 2, 2, 36)
        .transpose(3, 4, 2, 1, 0, 5)
        .reshape(2, wide // 2)
    )
    up_shift_own = jnp.where(zero, up_shift[0], up_shift[1])
    up_shift_other = jnp.where(zero, up_shift[1], up_shift[0])
    down_shift = small[:, 6 * rows + 36 :].reshape(width)

    def blocks_z(values):
        return values.reshape(values.shape[0], 4, width // 4).transpose(1, 0, 2)

    def unblock_z(blocks):
        return blocks.transpose(1, 0, 2).reshape(blocks.shape[1], width)

    def blocks_x(values):
        return (
            values.reshape(values.shape[0], 4, 4, HEAD)
            .transpose(2, 0, 1, 3)
            .reshape(4, values.shape[0], width // 4)
        )

    def unblock_x(blocks):
        count = blocks.shape[1]
        return blocks.reshape(4, count, 4, HEAD).transpose(1, 2, 0, 3).reshape(count, width)

    def blocks_y(values):
        return values.reshape(values.shape[0], 4, values.shape[1] // 4).transpose(1, 0, 2)

    def unblock_y(blocks):
        return blocks.transpose(1, 0, 2).reshape(blocks.shape[1], 4 * blocks.shape[2])

    def heads_of(values):
        return values.reshape(values.shape[0], heads, HEAD)

    def flat(values):
        return values.reshape(values.shape[0], width)

    def other_half(values):
        return lax.ppermute(values, "u", [(0, 1), (1, 0)])

    words = jnp.concatenate([text, other_half(text)], 0)
    word_blocks = (
        words.reshape(words.shape[0], 4, 4, 2, 2, 2, text_rows)
        .transpose(4, 5, 3, 0, 2, 1, 6)
        .reshape(2, 4, words.shape[0], 16 * text_rows)
    )
    words_own = jnp.where(zero, word_blocks[0], word_blocks[1])
    words_other = jnp.where(zero, word_blocks[1], word_blocks[0])

    resid = inputs.astype(F32)
    first = normalize(resid, gains[0], shifts[0]).astype(BF)
    first_blocks = blocks_z(first)
    own = joined_set.times(first_blocks, False).astype(BF)
    other = joined_set.times(first_blocks, True).astype(BF)
    query_key = jnp.where(zero, own, other)
    values_local = jnp.where(zero, other, own)[:, :width]
    queries = heads_of(query_key[:, :width])
    key_value = jnp.concatenate([query_key[:, width:], values_local], 1)
    key_value = jnp.concatenate([key_value, other_half(key_value)], 0)
    keys = heads_of(key_value[:, :width])
    values = heads_of(key_value[:, width:])
    attended, self_total = attend(queries, keys, values, scale)
    attended = flat(attended)
    attended_blocks = blocks_x(attended)

    def mixed(blocks, columns):
        return (
            mixed_set.times(blocks, False, columns),
            mixed_set.times(blocks, True, columns),
        )

    mine, theirs = mixed(attended_blocks, slice(0, width))
    second = resid + jnp.where(zero, mine, theirs)
    second_in = normalize(second, gains[1], shifts[1]).astype(BF)
    second_blocks = blocks_z(second_in)
    cross_columns = slice(width, 2 * width)
    cross_queries = jnp.where(
        zero,
        joined_set.times(second_blocks, True, cross_columns),
        joined_set.times(second_blocks, False, cross_columns),
    ).astype(BF)
    projected = (
        low_set.times_rows(words_own, False, text_part)
        + low_set.times_rows(words_other, True, text_part)
    ).astype(BF)
    projected_blocks = blocks_x(projected)
    mine, theirs = mixed(projected_blocks, slice(None))
    memory = jnp.where(zero, theirs, mine).astype(BF)
    cross_keys = heads_of(memory[:, :width])
    cross_values = heads_of(memory[:, width:])
    cross_heads = heads_of(cross_queries)
    cross_out, cross_total = attend(cross_heads, cross_keys, cross_values, scale)
    cross_out = flat(cross_out)
    cross_blocks = blocks_x(cross_out)
    mine, theirs = mixed(cross_blocks, cross_columns)
    third = second + jnp.where(zero, mine, theirs)
    third_in = normalize(third, gains[2], shifts[2]).astype(BF)
    third_blocks = blocks_z(third_in)
    upward_own = up_set.times(third_blocks, False) + up_shift_own
    upward_other = up_set.times(third_blocks, True) + up_shift_other
    hidden_own = jax.nn.gelu(upward_own).astype(BF)
    hidden_other = jax.nn.gelu(upward_other).astype(BF)
    hidden_own_blocks = blocks_y(hidden_own)
    hidden_other_blocks = blocks_y(hidden_other)
    final = (
        third
        + low_set.times_rows(hidden_own_blocks, False, down_part)
        + low_set.times_rows(hidden_other_blocks, True, down_part)
        + down_shift
    )
    block_output = final.astype(BF)

    pulled = cot.astype(F32) * masked.astype(F32)[:, None]
    branch = pulled.astype(BF)
    down_shift_grad = jnp.sum(branch.astype(F32), 0)
    hidden_both = jnp.concatenate([hidden_own_blocks, swap(hidden_other_blocks)], 1)
    branch_both = jnp.concatenate([branch, swap(branch)], 0)
    down_pieces = gradient_pieces(hidden_both, branch_both, "y")

    hidden_grad_own = unblock_y(low_set.back_rows(branch, False, down_part))
    hidden_grad_other = unblock_y(low_set.back_rows(branch, True, down_part))
    upward_grad_own = jax.vjp(jax.nn.gelu, upward_own)[1](hidden_grad_own)[0].astype(BF)
    upward_grad_other = jax.vjp(jax.nn.gelu, upward_other)[1](hidden_grad_other)[0].astype(BF)
    up_shift_grad_own = jnp.sum(upward_grad_own.astype(F32), 0)
    up_shift_grad_other = jnp.sum(upward_grad_other.astype(F32), 0)
    third_both = jnp.concatenate([third_blocks, swap(third_blocks)], 1)
    upward_grad_both = jnp.concatenate([upward_grad_own, swap(upward_grad_other)], 0)
    up_pieces = gradient_pieces(third_both, upward_grad_both, "z")
    third_in_grad = unblock_z(up_set.back(upward_grad_own, upward_grad_other))
    third_norm_grad, gain_two, shift_two = norm_back(third, gains[2], shifts[2], third_in_grad)
    third_grad = pulled + third_norm_grad
    cross_branch = third_grad.astype(BF)

    def mixed_back(value, columns):
        return unblock_x(
            by_place(
                [
                    jnp.where(
                        zero,
                        dot_nt(value, mixed_set.own[index][:, columns]),
                        dot_nt(value, mixed_set.other[mate][:, columns]),
                    )
                    for index, mate in enumerate((0, 2, 1, 3))
                ],
                mixed_set.own_spots,
            )
        )

    cross_out_grad = heads_of(mixed_back(cross_branch, cross_columns).astype(BF))
    cross_query_grad, cross_key_grad, cross_value_grad = attend_back(
        cross_heads, cross_keys, cross_values, cross_total, cross_out_grad, scale
    )
    memory_terms = jnp.concatenate([flat(cross_key_grad), flat(cross_value_grad)], 1).astype(BF)
    half_words = text.shape[0]
    memory_grad = (
        memory_terms[:half_words].astype(F32) + other_half(memory_terms[half_words:]).astype(F32)
    ).astype(BF)
    projected_grad = unblock_x(
        by_place(
            [
                jnp.where(
                    zero,
                    dot_nt(memory_grad, mixed_set.other[mate]),
                    dot_nt(memory_grad, mixed_set.own[index]),
                )
                for index, mate in enumerate((0, 2, 1, 3))
            ],
            mixed_set.own_spots,
        )
    ).astype(BF)
    query_flat = flat(cross_query_grad)
    second_in_grad = unblock_z(
        by_place(
            [
                jnp.where(
                    zero,
                    dot_nt(query_flat, joined_set.other[mate][:, cross_columns]),
                    dot_nt(query_flat, joined_set.own[index][:, cross_columns]),
                )
                for index, mate in enumerate((0, 2, 1, 3))
            ],
            joined_set.own_spots,
        )
    )
    second_norm_grad, gain_one, shift_one = norm_back(second, gains[1], shifts[1], second_in_grad)
    second_grad = third_grad + second_norm_grad
    self_branch = second_grad.astype(BF)
    attended_grad = heads_of(mixed_back(self_branch, slice(0, width)).astype(BF))
    query_grad, key_grad, value_grad = attend_back(
        queries, keys, values, self_total, attended_grad, scale
    )
    key_value_grad = jnp.concatenate([flat(key_grad), flat(value_grad)], 1).astype(BF)
    key_value_grad = (
        key_value_grad[:tokens].astype(F32) + other_half(key_value_grad[tokens:]).astype(F32)
    ).astype(BF)
    query_key_grad = jnp.concatenate([flat(query_grad), key_value_grad[:, :width]], 1)
    value_only = key_value_grad[:, width:]
    blank = jnp.zeros_like(value_only)
    value_blank = jnp.concatenate([value_only, blank], 1)
    first_grad = unblock_z(
        joined_set.back(
            jnp.where(zero, query_key_grad, value_blank),
            jnp.where(zero, value_blank, query_key_grad),
        )
    )
    input_norm_grad, gain_zero, shift_zero = norm_back(resid, gains[0], shifts[0], first_grad)
    input_grads = second_grad + input_norm_grad

    query_lefts, query_rights = pair(first_blocks, query_key_grad[:, :width], first_blocks, value_only)
    key_lefts, key_rights = pair(first_blocks, query_key_grad[:, width:], second_blocks, query_flat)
    joined_pieces = [
        jnp.concatenate([one, two], 1)
        for one, two in zip(
            gradient_pieces(query_lefts, query_rights, "z"),
            gradient_pieces(key_lefts, key_rights, "z"),
        )
    ]

    def padded(values):
        return jnp.concatenate(
            [values, jnp.zeros(values.shape[:-2] + (tokens - values.shape[-2], values.shape[-1]), BF)], -2
        )

    word_feature = padded(projected_blocks[:, :half_words])
    out_lefts, out_rights = pair(
        attended_blocks, self_branch, word_feature, padded(memory_grad[:, :width])
    )
    cross_lefts, cross_rights = pair(
        cross_blocks, cross_branch, word_feature, padded(memory_grad[:, width:])
    )
    mixed_pieces = [
        jnp.concatenate([one, two], 1)
        for one, two in zip(
            gradient_pieces(out_lefts, out_rights, "x"),
            gradient_pieces(cross_lefts, cross_rights, "x"),
        )
    ]
    text_lefts = jnp.concatenate(
        [words_own[:, :half_words], swap(words_other[:, :half_words])], 1
    )
    text_rights = jnp.concatenate([projected_grad, swap(projected_grad)], 0)
    text_pieces = gradient_pieces(text_lefts, text_rights, "y")

    def low_finish(pieces, count):
        part = scatter(pieces, "y")
        part = scatter_blocks(part.reshape(4, 4 * count, width), "x")
        return scatter_blocks(part.reshape(4, count, width), "z")

    down_total = low_finish(down_pieces, down_rows)
    text_total = low_finish(text_pieces, text_rows)

    def row_finish(part, axis):
        part = scatter_blocks(part.reshape(4, 8 * rows, -1), axis)
        part = (
            part.reshape(2, 2, 2, rows, -1).transpose(2, 0, 1, 3, 4).reshape(4, 2 * rows, -1)
        )
        part = scatter_blocks(part, "y").reshape(2, rows, -1)
        kept = jnp.where(zero, part[0], part[1])
        came = swap(jnp.where(zero, part[1], part[0]))
        return jnp.where(zero, kept, came), jnp.where(zero, came, kept)

    up_zero, up_one = row_finish(scatter(up_pieces, "z"), "x")
    up_total = (
        jnp.stack([up_zero, up_one], 1)
        .reshape(rows, 2, 2, 2, 4, 4, 36)
        .transpose(0, 5, 4, 3, 1, 2, 6)
        .reshape(rows, wide)
    )
    mixed_zero, mixed_one = row_finish(scatter(mixed_pieces, "x"), "z")
    out_total, cross_total_grad = mixed_zero[:, :width], mixed_zero[:, width:]
    memory_total = mixed_one
    joined_zero, joined_one = row_finish(scatter(joined_pieces, "z"), "x")
    joined_total = jnp.concatenate([joined_zero, joined_one[:, :width]], 1)
    query_total = joined_one[:, width:]

    up_shift_grad = (
        jnp.stack(
            [
                jnp.where(zero, up_shift_grad_own, up_shift_grad_other),
                jnp.where(zero, up_shift_grad_other, up_shift_grad_own),
            ]
        )
        .reshape(2, 2, 2, 4, 4, 36)
        .transpose(4, 3, 2, 0, 1, 5)
        .reshape(128, 36)
    )
    gain_terms = jnp.stack([gain_zero, gain_one, gain_two])
    shift_terms = jnp.stack([shift_zero, shift_one, shift_two])
    small_grads = jnp.concatenate(
        [
            gain_terms.reshape(3, 128, rows).transpose(1, 0, 2).reshape(128, 3 * rows),
            shift_terms.reshape(3, 128, rows).transpose(1, 0, 2).reshape(128, 3 * rows),
            up_shift_grad,
            down_shift_grad.reshape(128, rows),
        ],
        1,
    )
    small_total = jnp.sum(lax.all_to_all(small_grads, AXES, 0, 0, tiled=True), 0)
    gain_total = small_total[: 3 * rows].reshape(3, rows)
    shift_total = small_total[3 * rows : 6 * rows].reshape(3, rows)
    up_shift_total = small_total[6 * rows : 6 * rows + 36]
    down_shift_total = small_total[6 * rows + 36 :]
    return (
        block_output[None],
        input_grads[None],
        gain_total,
        shift_total,
        joined_total,
        out_total,
        text_total,
        query_total,
        memory_total,
        cross_total_grad,
        up_total,
        up_shift_total,
        down_total,
        down_shift_total,
    )


def solution(mesh):
    fine = Mesh(mesh.devices.reshape(4, 4, 2, 2, 2), AXES)
    tokens = P(DP, "u", None)
    split_rows = P(AXES, None)
    split_columns = P(None, AXES)
    split_vector = P(AXES)
    return jax.shard_map(
        per_device,
        mesh=fine,
        in_specs=(tokens, tokens, P(DP, "u"), tokens)
        + (split_columns,) * 2
        + (split_rows,) * 7
        + (split_vector, split_rows, split_vector),
        out_specs=(tokens, tokens)
        + (split_columns,) * 2
        + (split_rows,) * 7
        + (split_vector, split_rows, split_vector),
        check_vma=False,
    )
```

time: 4530 us -> 1010 us (0.22)
  waiting for transfers between devices: 2500 us -> 254 us
  blocking collectives: 1480 us -> 0 us
  matrix products: 132 us -> 260 us
  other arithmetic: 12.8 us -> 77.6 us
    all_gather x8 -> x0, waiting for transfers between devices: 1740 us -> none  [the longest x1 317 us: per_device(): lax.all_gather(w_qkv, ('dp', 'blk'), axis=0, tiled=True)]
    unnamed x3 -> x0, blocking collectives: 832 us -> none
    unnamed x49 -> x0, waiting for transfers between devices: 764 us -> none
    all_gather x5 -> x0, blocking collectives: 653 us -> none  [the longest x1 312 us: per_device(): lax.all_gather(norm_biases, ('dp', 'blk'), axis=1, tiled=True)]
    ppermute x0 -> x114, waiting for transfers between devices: none -> 254 us  [the longest x76 247 us: receive(): return lax.ppermute(value, NAMES[axis], pairs)]
    ppermute x0 -> x114, starting transfers between devices: none -> 180 us  [the longest x76 112 us: receive(): return lax.ppermute(value, NAMES[axis], pairs)]
    unnamed x36 -> x0, starting transfers between devices: 173 us -> none
    unnamed x197 -> x496, local copies, waits for them, and re-layouts: 186 us -> 19.7 us
  transfers between devices with their start and end apart: 45 -> 116, of which waited for: 9 -> 38; matrix products, arithmetic and copies ran while one was open for 21% -> 52% of each run, Pallas kernels for 0% -> 0%
where the time goes in v1:
time: 1010 us; the launch traced here: 993 us
  matrix products  260 us (26%)
  waiting for transfers between devices  254 us (25%)
  local copies, waits for them, and re-layouts  199 us (20%)
  starting transfers between devices  197 us (20%)
  other arithmetic  77.6 us (8%)
    ppermute x76, waiting for transfers between devices, receive(): return lax.ppermute(value, NAMES[axis], pairs)  247 us
    ppermute x76, starting transfers between devices, receive(): return lax.ppermute(value, NAMES[axis], pairs)  112 us
    dot_general x64, matrix products, dot(): return jnp.dot(left, right, preferred_element_type=F32)  108 us
    broadcast_in_dim x109, local copies, waits for them, and re-layouts, by_place(): out = jnp.where(slots == spot, piece[None], out)  93 us
    dot_general x56, matrix products, dot_nt(): lax.dot_general(left, right, (((1,), (1,)), ((), ())), preferred_element_...  90 us
    ppermute x34, starting transfers between devices, swap(): return lax.ppermute(value, 'c', [(0, 1), (1, 0)])  58.4 us
    dot_general x28, matrix products, dot_tn(): lax.dot_general(left, right, (((0,), (0,)), ((), ())), preferred_element_...  52.6 us
  transfers between devices with their start and end apart: 116, of which 38 were waited for; matrix products, arithmetic and copies ran while one was open for 52% of the time, Pallas kernels for 0%

profile of v1, /device:TPU:1, one launch (start us, length us, event | category | flops | bytes accessed | tf_op | source)
XLA Modules:
  0.0 993.4 jit_solution(16465527542295184195)
XLA Ops:
  3.8 4.6 collective-permute-start.28
  13.9 8.5 all-to-all-start
  70.1 4.3 collective-permute-done.2
  104.7 8.8 collective-permute-done.4
  113.6 7.4 collective-permute-done.5
  121.0 8.6 collective-permute-done.6
  135.8 16.1 %collective-permute-start.11 = (bf16[288,2304]{1,0:T(8,128)(2,1)}, bf16[288,2304]{1,0:T(8,128)(2,1)}, u32[]{:S(2)}, u32[]{:S(2)}) collective-permute-start(bf16[288,2304]{1,0:T(8,128)(2,1)} %get-tuple-element.52), channel_id=1, source_target_pairs={{0,2},{2,0},{1,3},{3,1},{4,6},{6,4},{5,7},{7,5},{8,10},{10,8},{9,1... | collective-permute-start | bytes 3981320 | tf_op jit(solution)/shard_map/ppermute | solution.py:60
  159.9 11.0 %collective-permute-done.19 = bf16[288,2304]{1,0:T(8,128)(2,1)} collective-permute-done((bf16[288,2304]{1,0:T(8,128)(2,1)}, bf16[288,2304]{1,0:T(8,128)(2,1)}, u32[]{:S(2)}, u32[]{:S(2)}) %collective-permute-start.19) | collective-permute-done | bytes 1327136 | tf_op jit(solution)/shard_map/ppermute | solution.py:77
  193.9 9.8 collective-permute-done.42
  203.6 4.1 collective-permute-start.37
  215.9 10.4 %collective-permute-done.9 = bf16[144,2304]{1,0:T(8,128)(2,1)S(1)} collective-permute-done((bf16[144,2304]{1,0:T(8,128)(2,1)S(1)}, bf16[144,2304]{1,0:T(8,128)(2,1)S(1)}, u32[]{:S(2)}, u32[]{:S(2)}) %collective-permute-start.9) | collective-permute-done | bytes 663584 | tf_op jit(solution)/shard_map/ppermute | solution.py:77
  233.3 6.2 collective-permute-done.44
  239.5 8.0 collective-permute-start.104
  284.3 14.7 %collective-permute-done.36 = bf16[544,1152]{1,0:T(8,128)(2,1)S(1)} collective-permute-done((bf16[544,1152]{1,0:T(8,128)(2,1)}, bf16[544,1152]{1,0:T(8,128)(2,1)S(1)}, u32[]{:S(2)}, u32[]{:S(2)}) %collective-permute-start.36) | collective-permute-done | bytes 1253408 | tf_op jit(solution)/shard_map/ppermute | solution.py:77
  303.8 3.8 collective-permute-start.15
  316.2 5.2 collective-permute-done.15
  423.7 5.3 convert_reduce_fusion
  668.5 8.8 all-to-all-start.1
  708.7 9.5 collective-permute-done.84
  727.4 10.1 %collective-permute-done.85 = bf16[128,1152]{1,0:T(8,128)(2,1)S(1)} collective-permute-done((bf16[128,1152]{1,0:T(8,128)(2,1)S(1)}, bf16[128,1152]{1,0:T(8,128)(2,1)S(1)}, u32[]{:S(2)}, u32[]{:S(2)}) %collective-permute-start.85) | collective-permute-done | bytes 294944 | tf_op jit(solution)/shard_map/ppermute | solution.py:77
  739.1 6.9 collective-permute-done.87
  765.4 8.5 collective-permute-done.72
  782.8 24.2 %collective-permute-done.107 = bf16[576,1152]{1,0:T(8,128)(2,1)S(1)} collective-permute-done((bf16[576,1152]{1,0:T(8,128)(2,1)S(1)}, bf16[576,1152]{1,0:T(8,128)(2,1)S(1)}, u32[]{:S(2)}, u32[]{:S(2)}) %collective-permute-start.107) | collective-permute-done | bytes 1327136 | tf_op jit(solution)/shard_map/ppermute | solution.py:77
  818.1 4.5 collective-permute-done.73
  822.6 41.1 %collective-permute-done.74 = bf16[72,2304]{1,0:T(8,128)(2,1)S(1)} collective-permute-done((bf16[72,2304]{1,0:T(8,128)(2,1)S(1)}, bf16[72,2304]{1,0:T(8,128)(2,1)S(1)}, u32[]{:S(2)}, u32[]{:S(2)}) %collective-permute-start.74) | collective-permute-done | bytes 331808 | tf_op jit(solution)/shard_map/ppermute | solution.py:77
  873.5 14.3 %collective-permute-start.109 = (bf16[144,1152]{1,0:T(8,128)(2,1)}, bf16[144,1152]{1,0:T(8,128)(2,1)S(1)}, u32[]{:S(2)}, u32[]{:S(2)}) collective-permute-start(bf16[144,1152]{1,0:T(8,128)(2,1)} %get-tuple-element.41), channel_id=1, source_target_pairs={{8,0},{16,8},{24,16},{0,24},{26,2},{2,10},{10,18},{18,26},{9,1},{1... | collective-permute-start | bytes 995336 | tf_op jit(solution)/shard_map/ppermute | solution.py:77
  887.9 9.0 collective-permute-start.79
  900.7 7.7 collective-permute-done.110
  916.9 5.3 collective-permute-done.98
  929.7 13.5 %collective-permute-done.57 = bf16[288,2304]{1,0:T(8,128)(2,1)} collective-permute-done((bf16[288,2304]{1,0:T(8,128)(2,1)}, bf16[288,2304]{1,0:T(8,128)(2,1)}, u32[]{:S(2)}, u32[]{:S(2)}) %collective-permute-start.57) | collective-permute-done | bytes 1327136 | tf_op jit(solution)/shard_map/ppermute | solution.py:77
  943.1 4.1 collective-permute-start.99
  965.7 8.7 collective-permute-done.60
  (1233 shorter events, 674.6 us)
Async XLA Ops:
  3.8 80.5 %collective-permute-start.28 = (bf16[68,1152]{1,0:T(8,128)(2,1)}, bf16[68,1152]{1,0:T(8,128)(2,1)}, u32[]{:S(2)}, u32[]{:S(2)}) collective-permute-start(bf16[68,1152]{1,0:T(8,128)(2,1)} %constant_dynamic-update-slice_fusion.4), channel_id=1, source_target_pairs={{96,0},{0,32},{32,64},{64,96},{34,2},{66,34},{98,66},{2,98},{97,1}... | collective-permute-start | bytes 470024 | tf_op jit(solution)/shard_map/ppermute | solution.py:77
  8.4 77.4 %collective-permute-start.29 = (bf16[68,1152]{1,0:T(8,128)(2,1)}, bf16[68,1152]{1,0:T(8,128)(2,1)}, u32[]{:S(2)}, u32[]{:S(2)}) collective-permute-start(bf16[68,1152]{1,0:T(8,128)(2,1)} %constant_dynamic-update-slice_fusion.4), channel_id=1, source_target_pairs={{32,0},{64,32},{96,64},{0,96},{98,2},{2,34},{34,66},{66,98},{33,1}... | collective-permute-start | bytes 470024 | tf_op jit(solution)/shard_map/ppermute | solution.py:77
  87.5 45.1 %collective-permute-start.31 = (bf16[272,1152]{1,0:T(8,128)(2,1)S(1)}, bf16[272,1152]{1,0:T(8,128)(2,1)S(1)}, u32[]{:S(2)}, u32[]{:S(2)}) collective-permute-start(bf16[272,1152]{1,0:T(8,128)(2,1)S(1)} %pad_maximum_fusion.9), channel_id=1, source_target_pairs={{24,0},{0,8},{8,16},{16,24},{10,2},{18,10},{26,18},{2,26},{25,1},{... | collective-permute-start | bytes 1880072 | tf_op jit(solution)/shard_map/ppermute | solution.py:77
  90.0 45.7 %collective-permute-start.32 = (bf16[272,1152]{1,0:T(8,128)(2,1)S(1)}, bf16[272,1152]{1,0:T(8,128)(2,1)S(1)}, u32[]{:S(2)}, u32[]{:S(2)}) collective-permute-start(bf16[272,1152]{1,0:T(8,128)(2,1)S(1)} %pad_maximum_fusion.9), channel_id=1, source_target_pairs={{8,0},{16,8},{24,16},{0,24},{26,2},{2,10},{10,18},{18,26},{9,1},{1... | collective-permute-start | bytes 1880072 | tf_op jit(solution)/shard_map/ppermute | solution.py:77
  121.0 49.9 %collective-permute-start.19 = (bf16[288,2304]{1,0:T(8,128)(2,1)}, bf16[288,2304]{1,0:T(8,128)(2,1)}, u32[]{:S(2)}, u32[]{:S(2)}) collective-permute-start(bf16[288,2304]{1,0:T(8,128)(2,1)} %fusion.51), channel_id=1, source_target_pairs={{8,0},{16,8},{24,16},{0,24},{26,2},{2,10},{10,18},{18,26},{9,1},{1... | collective-permute-start | bytes 3981320 | tf_op jit(solution)/shard_map/ppermute | solution.py:77
  129.6 43.6 %collective-permute-start.20 = (bf16[288,2304]{1,0:T(8,128)(2,1)}, bf16[288,2304]{1,0:T(8,128)(2,1)}, u32[]{:S(2)}, u32[]{:S(2)}) collective-permute-start(bf16[288,2304]{1,0:T(8,128)(2,1)} %fusion.51), channel_id=1, source_target_pairs={{24,0},{0,8},{8,16},{16,24},{10,2},{18,10},{26,18},{2,26},{25,1},{... | collective-permute-start | bytes 3981320 | tf_op jit(solution)/shard_map/ppermute | solution.py:77
  132.6 46.6 %collective-permute-start.7 = (bf16[288,2304]{1,0:T(8,128)(2,1)}, bf16[288,2304]{1,0:T(8,128)(2,1)}, u32[]{:S(2)}, u32[]{:S(2)}) collective-permute-start(bf16[288,2304]{1,0:T(8,128)(2,1)} %get-tuple-element.52), channel_id=1, source_target_pairs={{32,0},{64,32},{96,64},{0,96},{98,2},{2,34},{34,66},{66,98},{33,1}... | collective-permute-start | bytes 3981320 | tf_op jit(solution)/shard_map/ppermute | solution.py:77
  135.8 45.3 %collective-permute-start.11 = (bf16[288,2304]{1,0:T(8,128)(2,1)}, bf16[288,2304]{1,0:T(8,128)(2,1)}, u32[]{:S(2)}, u32[]{:S(2)}) collective-permute-start(bf16[288,2304]{1,0:T(8,128)(2,1)} %get-tuple-element.52), channel_id=1, source_target_pairs={{0,2},{2,0},{1,3},{3,1},{4,6},{6,4},{5,7},{7,5},{8,10},{10,8},{9,1... | collective-permute-start | bytes 3981320 | tf_op jit(solution)/shard_map/ppermute | solution.py:60
  185.4 64.0 %collective-permute-start.34 = (bf16[1088,1152]{1,0:T(8,128)(2,1)}, bf16[1088,1152]{1,0:T(8,128)(2,1)}, u32[]{:S(2)}, u32[]{:S(2)}) collective-permute-start(bf16[1088,1152]{1,0:T(8,128)(2,1)} %pad_maximum_fusion), channel_id=1, source_target_pairs={{4,0},{1,4},{5,1},{0,5},{7,2},{2,6},{6,3},{3,7},{12,8},{9,12},{13,... | collective-permute-start | bytes 7520264 | tf_op jit(solution)/shard_map/ppermute | solution.py:77
  203.6 53.1 %collective-permute-start.37 = (bf16[1088,1152]{1,0:T(8,128)(2,1)}, bf16[1088,1152]{1,0:T(8,128)(2,1)}, u32[]{:S(2)}, u32[]{:S(2)}) collective-permute-start(bf16[1088,1152]{1,0:T(8,128)(2,1)} %pad_maximum_fusion), channel_id=1, source_target_pairs={{0,2},{2,0},{1,3},{3,1},{4,6},{6,4},{5,7},{7,5},{8,10},{10,8},{9,1... | collective-permute-start | bytes 7520264 | tf_op jit(solution)/shard_map/ppermute | solution.py:60
  239.5 369.7 %collective-permute-start.104 = (bf16[128,1152]{1,0:T(8,128)(2,1)}, bf16[128,1152]{1,0:T(8,128)(2,1)}, u32[]{:S(2)}, u32[]{:S(2)}) collective-permute-start(bf16[128,1152]{1,0:T(8,128)(2,1)} %get-tuple-element.31), channel_id=1, source_target_pairs={{0,2},{2,0},{1,3},{3,1},{4,6},{6,4},{5,7},{7,5},{8,10},{10,8},{9,1... | collective-permute-start | bytes 884744 | tf_op jit(solution)/shard_map/ppermute | solution.py:60
  248.5 335.9 %collective-permute-start.80 = (bf16[4,16,512]{2,1,0:T(8,128)(2,1)}, bf16[4,16,512]{2,1,0:T(8,128)(2,1)}, u32[]{:S(2)}, u32[]{:S(2)}) collective-permute-start(bf16[4,16,512]{2,1,0:T(8,128)(2,1)} %slice.587), channel_id=1, source_target_pairs={{0,2},{2,0},{1,3},{3,1},{4,6},{6,4},{5,7},{7,5},{8,10},{10,8},{9,1... | collective-permute-start | bytes 196616 | tf_op jit(solution)/shard_map/ppermute | solution.py:60
  271.0 61.4 %collective-permute-start.23 = (bf16[288,2304]{1,0:T(8,128)(2,1)}, bf16[288,2304]{1,0:T(8,128)(2,1)}, u32[]{:S(2)}, u32[]{:S(2)}) collective-permute-start(bf16[288,2304]{1,0:T(8,128)(2,1)} %fusion.51), channel_id=1, source_target_pairs={{0,2},{2,0},{1,3},{3,1},{4,6},{6,4},{5,7},{7,5},{8,10},{10,8},{9,1... | collective-permute-start | bytes 3981320 | tf_op jit(solution)/shard_map/ppermute | solution.py:60
  357.6 48.0 %collective-permute-start.46 = (bf16[288,2304]{1,0:T(8,128)(2,1)}, bf16[288,2304]{1,0:T(8,128)(2,1)}, u32[]{:S(2)}, u32[]{:S(2)}) collective-permute-start(bf16[288,2304]{1,0:T(8,128)(2,1)} %get-tuple-element.51), channel_id=1, source_target_pairs={{0,2},{2,0},{1,3},{3,1},{4,6},{6,4},{5,7},{7,5},{8,10},{10,8},{9,1... | collective-permute-start | bytes 3981320 | tf_op jit(solution)/shard_map/ppermute | solution.py:60
  363.6 55.2 %collective-permute-start.47 = (bf16[288,2304]{1,0:T(8,128)(2,1)}, bf16[288,2304]{1,0:T(8,128)(2,1)}, u32[]{:S(2)}, u32[]{:S(2)}) collective-permute-start(bf16[288,2304]{1,0:T(8,128)(2,1)} %copy-done.28), channel_id=1, source_target_pairs={{0,2},{2,0},{1,3},{3,1},{4,6},{6,4},{5,7},{7,5},{8,10},{10,8},{9,1... | collective-permute-start | bytes 3981320 | tf_op jit(solution)/shard_map/ppermute | solution.py:60
  371.3 43.6 %collective-permute-start.49 = (bf16[288,2304]{1,0:T(8,128)(2,1)}, bf16[288,2304]{1,0:T(8,128)(2,1)}, u32[]{:S(2)}, u32[]{:S(2)}) collective-permute-start(bf16[288,2304]{1,0:T(8,128)(2,1)} %constant_dynamic-update-slice_fusion.8), channel_id=1, source_target_pairs={{0,2},{2,0},{1,3},{3,1},{4,6},{6,4},{5,7},{7,5},{8,10},{10,8},{9,1... | collective-permute-start | bytes 3981320 | tf_op jit(solution)/shard_map/ppermute | solution.py:60
  486.1 50.2 %collective-permute-start.66 = (bf16[16,2304]{1,0:T(8,128)(2,1)}, bf16[16,2304]{1,0:T(8,128)(2,1)}, u32[]{:S(2)}, u32[]{:S(2)}) collective-permute-start(bf16[16,2304]{1,0:T(8,128)(2,1)} %slice.580), channel_id=1, source_target_pairs={{0,1},{1,0},{2,3},{3,2},{4,5},{5,4},{6,7},{7,6},{8,9},{9,8},{10,11... | collective-permute-start | bytes 221192 | tf_op jit(solution)/shard_map/ppermute | solution.py:307
  517.9 74.3 %collective-permute-start.65 = (bf16[4,128,288]{1,2,0:T(8,128)(2,1)}, bf16[4,128,288]{1,2,0:T(8,128)(2,1)}, u32[]{:S(2)}, u32[]{:S(2)}) collective-permute-start(bf16[4,128,288]{1,2,0:T(8,128)(2,1)} %get-tuple-element.81), channel_id=1, source_target_pairs={{0,2},{2,0},{1,3},{3,1},{4,6},{6,4},{5,7},{7,5},{8,10},{10,8},{9,1... | collective-permute-start | bytes 884744 | tf_op jit(solution)/shard_map/ppermute | solution.py:60
  518.4 75.6 %collective-permute-start.68 = (bf16[4,128,288]{1,2,0:T(8,128)(2,1)}, bf16[4,128,288]{1,2,0:T(8,128)(2,1)}, u32[]{:S(2)}, u32[]{:S(2)}) collective-permute-start(bf16[4,128,288]{1,2,0:T(8,128)(2,1)} %get-tuple-element.104), channel_id=1, source_target_pairs={{0,2},{2,0},{1,3},{3,1},{4,6},{6,4},{5,7},{7,5},{8,10},{10,8},{9,1... | collective-permute-start | bytes 884744 | tf_op jit(solution)/shard_map/ppermute | solution.py:60
  592.2 97.7 %collective-permute-start.51 = (bf16[4,128,288]{1,2,0:T(8,128)(2,1)}, bf16[4,128,288]{1,2,0:T(8,128)(2,1)}, u32[]{:S(2)}, u32[]{:S(2)}) collective-permute-start(bf16[4,128,288]{1,2,0:T(8,128)(2,1)} %fusion.749), channel_id=1, source_target_pairs={{0,2},{2,0},{1,3},{3,1},{4,6},{6,4},{5,7},{7,5},{8,10},{10,8},{9,1... | collective-permute-start | bytes 884744 | tf_op jit(solution)/shard_map/ppermute | solution.py:60
  592.3 106.9 %collective-permute-start.53 = (bf16[4,128,288]{1,2,0:T(8,128)(2,1)}, bf16[4,128,288]{1,2,0:T(8,128)(2,1)}, u32[]{:S(2)}, u32[]{:S(2)}) collective-permute-start(bf16[4,128,288]{1,2,0:T(8,128)(2,1)} %get-tuple-element.89), channel_id=1, source_target_pairs={{0,2},{2,0},{1,3},{3,1},{4,6},{6,4},{5,7},{7,5},{8,10},{10,8},{9,1... | collective-permute-start | bytes 884744 | tf_op jit(solution)/shard_map/ppermute | solution.py:60
  617.4 91.3 %collective-permute-start.82 = (bf16[512,1152]{1,0:T(8,128)(2,1)}, bf16[512,1152]{1,0:T(8,128)(2,1)}, u32[]{:S(2)}, u32[]{:S(2)}) collective-permute-start(bf16[512,1152]{1,0:T(8,128)(2,1)} %convolution_convert_fusion.8), channel_id=1, source_target_pairs={{5,0},{0,4},{4,1},{1,5},{6,2},{3,6},{7,3},{2,7},{13,8},{8,12},{12,... | collective-permute-start | bytes 3538952 | tf_op jit(solution)/shard_map/ppermute | solution.py:77
  619.3 89.4 %collective-permute-start.83 = (bf16[512,1152]{1,0:T(8,128)(2,1)}, bf16[512,1152]{1,0:T(8,128)(2,1)}, u32[]{:S(2)}, u32[]{:S(2)}) collective-permute-start(bf16[512,1152]{1,0:T(8,128)(2,1)} %convolution_convert_fusion.7), channel_id=1, source_target_pairs={{4,0},{1,4},{5,1},{0,5},{7,2},{2,6},{6,3},{3,7},{12,8},{9,12},{13,... | collective-permute-start | bytes 3538952 | tf_op jit(solution)/shard_map/ppermute | solution.py:77
  626.5 66.4 %collective-permute-start.52 = (bf16[128,1152]{1,0:T(8,128)(2,1)}, bf16[128,1152]{1,0:T(8,128)(2,1)}, u32[]{:S(2)}, u32[]{:S(2)}) collective-permute-start(bf16[128,1152]{1,0:T(8,128)(2,1)} %get-tuple-element.63), channel_id=1, source_target_pairs={{0,2},{2,0},{1,3},{3,1},{4,6},{6,4},{5,7},{7,5},{8,10},{10,8},{9,1... | collective-permute-start | bytes 884744 | tf_op jit(solution)/shard_map/ppermute | solution.py:60
  699.3 62.3 %collective-permute-start.70 = (bf16[288,2304]{1,0:T(8,128)(2,1)S(1)}, bf16[288,2304]{1,0:T(8,128)(2,1)S(1)}, u32[]{:S(2)}, u32[]{:S(2)}) collective-permute-start(bf16[288,2304]{1,0:T(8,128)(2,1)S(1)} %copy-done.102), channel_id=1, source_target_pairs={{24,0},{0,8},{8,16},{16,24},{10,2},{18,10},{26,18},{2,26},{25,1},{... | collective-permute-start | bytes 3981320 | tf_op jit(solution)/shard_map/ppermute | solution.py:77
  701.8 62.2 %collective-permute-start.71 = (bf16[288,2304]{1,0:T(8,128)(2,1)S(1)}, bf16[288,2304]{1,0:T(8,128)(2,1)S(1)}, u32[]{:S(2)}, u32[]{:S(2)}) collective-permute-start(bf16[288,2304]{1,0:T(8,128)(2,1)S(1)} %copy-done.101), channel_id=1, source_target_pairs={{8,0},{16,8},{24,16},{0,24},{26,2},{2,10},{10,18},{18,26},{9,1},{1... | collective-permute-start | bytes 3981320 | tf_op jit(solution)/shard_map/ppermute | solution.py:77
  761.6 45.4 %collective-permute-start.107 = (bf16[576,1152]{1,0:T(8,128)(2,1)S(1)}, bf16[576,1152]{1,0:T(8,128)(2,1)S(1)}, u32[]{:S(2)}, u32[]{:S(2)}) collective-permute-start(bf16[576,1152]{1,0:T(8,128)(2,1)S(1)} %copy-done.97), channel_id=1, source_target_pairs={{1,0},{5,4},{0,1},{4,5},{3,2},{7,6},{2,3},{6,7},{9,8},{13,12},{8,9... | collective-permute-start | bytes 3981320 | tf_op jit(solution)/shard_map/ppermute | solution.py:77
  763.9 47.3 %collective-permute-start.93 = (bf16[288,2304]{1,0:T(8,128)(2,1)S(1)}, bf16[288,2304]{1,0:T(8,128)(2,1)S(1)}, u32[]{:S(2)}, u32[]{:S(2)}) collective-permute-start(bf16[288,2304]{1,0:T(8,128)(2,1)S(1)} %copy-done.74), channel_id=1, source_target_pairs={{96,0},{0,32},{32,64},{64,96},{34,2},{66,34},{98,66},{2,98},{97,1}... | collective-permute-start | bytes 3981320 | tf_op jit(solution)/shard_map/ppermute | solution.py:77
  782.7 144.5 %collective-permute-start.55 = (bf16[288,2304]{1,0:T(8,128)(2,1)}, bf16[288,2304]{1,0:T(8,128)(2,1)}, u32[]{:S(2)}, u32[]{:S(2)}) collective-permute-start(bf16[288,2304]{1,0:T(8,128)(2,1)} %pad_maximum_fusion.1), channel_id=1, source_target_pairs={{96,0},{0,32},{32,64},{64,96},{34,2},{66,34},{98,66},{2,98},{97,1}... | collective-permute-start | bytes 3981320 | tf_op jit(solution)/shard_map/ppermute | solution.py:77
  806.9 120.4 %collective-permute-start.56 = (bf16[288,2304]{1,0:T(8,128)(2,1)}, bf16[288,2304]{1,0:T(8,128)(2,1)}, u32[]{:S(2)}, u32[]{:S(2)}) collective-permute-start(bf16[288,2304]{1,0:T(8,128)(2,1)} %pad_maximum_fusion.2), channel_id=1, source_target_pairs={{32,0},{64,32},{96,64},{0,96},{98,2},{2,34},{34,66},{66,98},{33,1}... | collective-permute-start | bytes 3981320 | tf_op jit(solution)/shard_map/ppermute | solution.py:77
  814.0 49.7 %collective-permute-start.74 = (bf16[72,2304]{1,0:T(8,128)(2,1)S(1)}, bf16[72,2304]{1,0:T(8,128)(2,1)S(1)}, u32[]{:S(2)}, u32[]{:S(2)}) collective-permute-start(bf16[72,2304]{1,0:T(8,128)(2,1)S(1)} %get-tuple-element.47), channel_id=1, source_target_pairs={{32,0},{64,32},{96,64},{0,96},{98,2},{2,34},{34,66},{66,98},{33,1}... | collective-permute-start | bytes 995336 | tf_op jit(solution)/shard_map/ppermute | solution.py:77
  814.0 49.7 %collective-permute-start.75 = (bf16[72,2304]{1,0:T(8,128)(2,1)S(1)}, bf16[72,2304]{1,0:T(8,128)(2,1)S(1)}, u32[]{:S(2)}, u32[]{:S(2)}) collective-permute-start(bf16[72,2304]{1,0:T(8,128)(2,1)S(1)} %get-tuple-element.46), channel_id=1, source_target_pairs={{64,0},{96,32},{0,64},{32,96},{66,2},{98,34},{2,66},{34,98},{65,1}... | collective-permute-start | bytes 995336 | tf_op jit(solution)/shard_map/ppermute | solution.py:77
  (326 other events, 3960.6 us)
